TPU v7x, 256 devices: a whole 4x4x8 slice. The times are simulated.
256 devices in a mesh: segment: 4 (over y_hi, core), frame: 64 (over x, z, y_lo).
Axes of the slice: x: 4, y: 4 (y_hi: 2, y_lo: 2; y = y_hi * 2 + y_lo), z: 8, core: 2. Of those that a mesh axis runs over, the one named last changes fastest.
Arguments:
- clips: bfloat16 [4, 64, 320, 1024], P('segment', 'frame'), may hold values from -6 to 6
- timesteps: int32 [4], replicated, may hold values from 0 to 999
- gain: float32 [4, 320], replicated, may hold values from 0.25 to 1.75
- temporal_weight: bfloat16 [4, 3, 320, 320], P('segment'), may hold values from -0.1875 to 0.1875
- film_weight: bfloat16 [4, 320, 320], P('segment'), may hold values from -0.3125 to 0.3125
- out_weight: bfloat16 [4, 320, 320], P('segment'), may hold values from -0.3125 to 0.3125
- skip_weight: bfloat16 [2, 320, 320], replicated, may hold values from -0.3125 to 0.3125
Outputs:
- video_out: bfloat16 [4, 64, 320, 1024], P('segment', 'frame')
All inputs are finite; a program needn't handle non-finite values.
Results may differ from a plain program's by a relative error of at most 0.012.
Values may be sent and summed in bfloat16 or wider, within the bound.
A program may use at most 64 MiB of HBM per device.

v0:
```python
import math
import jax
import jax.numpy as jnp
from jax import lax
from jax.sharding import PartitionSpec as P


def extended(cells, sides, width):
    for axis, dim in sides:
        count = lax.axis_size(axis)
        ends = count - 1
        head = lax.slice_in_dim(cells, 0, width, axis=dim)
        tail = lax.slice_in_dim(cells, cells.shape[dim] - width, cells.shape[dim], axis=dim)
        cells = jnp.concatenate(
            [
                lax.ppermute(tail, axis, [(i, (i + 1) % count) for i in range(ends)]),
                cells,
                lax.ppermute(head, axis, [((i + 1) % count, i) for i in range(ends)]),
            ],
            axis=dim,
        )
    return cells


def shifted(array, axis, by):
    length = lax.axis_size(axis)
    pairs = [(i, i + by) for i in range(length) if 0 <= i + by < length]
    return lax.ppermute(array, axis, pairs)


def embed(timesteps, width):
    half = width // 2
    freq = jnp.exp(-math.log(10000.0) * jnp.arange(half, dtype=jnp.float32) / half)
    angle = timesteps.astype(jnp.float32)[:, None] * freq[None, :]
    return jnp.concatenate([jnp.sin(angle), jnp.cos(angle)], axis=-1).astype(jnp.bfloat16)


def channel_mix(weight, field):
    return jnp.einsum("io,fip->fop", weight, field, preferred_element_type=jnp.float32)


def temporal_mix(normed, taps):
    padded = extended(normed, (("frame", 0),), 1)
    count = normed.shape[0]
    mixed = channel_mix(taps[0], padded[0:count])
    mixed = mixed + channel_mix(taps[1], padded[1 : count + 1])
    mixed = mixed + channel_mix(taps[2], padded[2 : count + 2])
    return mixed


def section_core(state, own_gain, taps, film_vec, projection):
    values = state.astype(jnp.float32)
    meansq = jnp.mean(values * values, axis=1, keepdims=True)
    normed = (values * lax.rsqrt(meansq + 1e-05) * own_gain[None, :, None]).astype(jnp.bfloat16)
    mixed = temporal_mix(normed, taps)
    hidden = jax.nn.silu(mixed * (1.0 + film_vec[None, :, None])).astype(jnp.bfloat16)
    return values + channel_mix(projection, hidden)


def shards(clips, timesteps, gain, temporal_weight, film_weight, out_weight, skip_weight):
    sections = lax.axis_size("segment")
    section = lax.axis_index("segment")
    emb = embed(timesteps, clips.shape[2])
    all_clips = lax.all_gather(clips, "segment", axis=0, tiled=True)
    batches = all_clips.shape[0]
    film_all = jnp.dot(emb, film_weight[0], preferred_element_type=jnp.float32)
    own_gain = lax.dynamic_index_in_dim(gain, section, 0, keepdims=False)
    taps = temporal_weight[0]
    projection = out_weight[0]
    decoder_weight = jnp.where(section == sections - 1, skip_weight[1], skip_weight[0])
    is_first = section == 0
    is_decoder = section >= 2
    empty = jnp.zeros(all_clips.shape[1:], jnp.bfloat16)
    handed = empty
    carried = empty
    finals = []
    steps_total = batches + sections - 1
    for step in range(steps_total):
        source = all_clips[step] if step < batches else empty
        state = jnp.where(is_first, source, handed)
        micro = step - section
        select = jnp.arange(batches) == micro
        film_vec = jnp.sum(jnp.where(select[:, None], film_all, 0.0), axis=0)
        far_skip = empty
        if step >= 3 and step - 3 < batches:
            far_skip = all_clips[step - 3]
        skip_in = jnp.where(section == sections - 1, far_skip, carried)
        total = section_core(state, own_gain, taps, film_vec, projection)
        skip_term = channel_mix(decoder_weight, skip_in)
        total = total + jnp.where(is_decoder, skip_term, 0.0)
        result = total.astype(jnp.bfloat16)
        if step >= sections - 1:
            finals.append(result)
        if step < steps_total - 1:
            handed, carried = shifted((result, state), "segment", 1)
    stacked = jnp.stack(finals, axis=0).astype(jnp.float32)
    stacked = jnp.where(section == sections - 1, stacked, 0.0)
    return lax.psum_scatter(
        stacked.astype(jnp.bfloat16), "segment", scatter_dimension=0, tiled=True
    )


def solution(mesh):
    placed = (
        P("segment", "frame", None, None),
        P(),
        P(),
        P("segment", None, None, None),
        P("segment", None, None),
        P("segment", None, None),
        P(),
    )
    return jax.shard_map(
        shards,
        mesh=mesh,
        in_specs=placed,
        out_specs=P("segment", "frame", None, None),
        check_vma=False,
    )
```

profile of v0, /device:TPU:1, one launch (start us, length us, event | category | flops | bytes accessed | tf_op | source)
XLA Modules:
  0.0 453.3 jit_solution(10235497476458363797)
XLA Ops:
  10.0 35.6 %all-gather.2.cloned.1.call-done = bf16[4,1,320,1024]{3,2,1,0:T(8,128)(2,1)} async-done(((bf16[1,1,320,1024]{3,2,1,0:T(8,128)(2,1)}), bf16[4,1,320,1024]{3,2,1,0:T(8,128)(2,1)}) %all-gather.2.cloned.1.call-update) | async-done | bytes 2621456 | tf_op jit(solution)/shard_map/all_gather | solution.py:64
  56.3 8.7 %collective-permute-done.1 = bf16[1,320,1024]{2,1,0:T(8,128)(2,1)S(1)} collective-permute-done((bf16[1,320,1024]{2,1,0:T(8,128)(2,1)S(1)}, bf16[1,320,1024]{2,1,0:T(8,128)(2,1)S(1)}, u32[]{:S(2)}, u32[]{:S(2)}) %collective-permute-start.1) | collective-permute-done | bytes 655392 | tf_op jit(solution)/shard_map/ppermute | solution.py:18
  66.7 12.0 %collective-permute-done = bf16[1,320,1024]{2,1,0:T(8,128)(2,1)} collective-permute-done((bf16[1,320,1024]{2,1,0:T(8,128)(2,1)S(1)}, bf16[1,320,1024]{2,1,0:T(8,128)(2,1)}, u32[]{:S(2)}, u32[]{:S(2)}) %collective-permute-start) | collective-permute-done | bytes 655392 | tf_op jit(solution)/shard_map/ppermute | solution.py:16
  88.2 5.5 %collective-permute-done.2 = bf16[1,320,1024]{2,1,0:T(8,128)(2,1)S(1)} collective-permute-done((bf16[1,320,1024]{2,1,0:T(8,128)(2,1)S(1)}, bf16[1,320,1024]{2,1,0:T(8,128)(2,1)S(1)}, u32[]{:S(2)}, u32[]{:S(2)}) %collective-permute-start.2) | collective-permute-done | bytes 655392 | tf_op jit(solution)/shard_map/ppermute | solution.py:28
  96.7 5.9 %collective-permute-start.3 = (bf16[1,320,1024]{2,1,0:T(8,128)(2,1)S(1)}, bf16[1,320,1024]{2,1,0:T(8,128)(2,1)}, u32[]{:S(2)}, u32[]{:S(2)}) collective-permute-start(bf16[1,320,1024]{2,1,0:T(8,128)(2,1)S(1)} %fusion.54), channel_id=1, source_target_pairs={{0,1},{1,2},{2,3},{3,4},{4,5},{5,6},{6,7},{7,8},{8,9},{9,10},{10,1... | collective-permute-start | bytes 1966088 | tf_op jit(solution)/shard_map/ppermute | solution.py:16
  102.5 17.2 %collective-permute-done.5 = bf16[1,320,1024]{2,1,0:T(8,128)(2,1)S(1)} collective-permute-done((bf16[1,320,1024]{2,1,0:T(8,128)(2,1)S(1)}, bf16[1,320,1024]{2,1,0:T(8,128)(2,1)S(1)}, u32[]{:S(2)}, u32[]{:S(2)}) %collective-permute-start.5) | collective-permute-done | bytes 655392 | tf_op jit(solution)/shard_map/ppermute | solution.py:28
  136.2 5.6 %collective-permute-done.6 = bf16[1,320,1024]{2,1,0:T(8,128)(2,1)S(1)} collective-permute-done((bf16[1,320,1024]{2,1,0:T(8,128)(2,1)S(1)}, bf16[1,320,1024]{2,1,0:T(8,128)(2,1)S(1)}, u32[]{:S(2)}, u32[]{:S(2)}) %collective-permute-start.6) | collective-permute-done | bytes 655392 | tf_op jit(solution)/shard_map/ppermute | solution.py:28
  144.7 6.2 %collective-permute-start.7 = (bf16[1,320,1024]{2,1,0:T(8,128)(2,1)S(1)}, bf16[1,320,1024]{2,1,0:T(8,128)(2,1)}, u32[]{:S(2)}, u32[]{:S(2)}) collective-permute-start(bf16[1,320,1024]{2,1,0:T(8,128)(2,1)S(1)} %fusion.57), channel_id=1, source_target_pairs={{0,1},{1,2},{2,3},{3,4},{4,5},{5,6},{6,7},{7,8},{8,9},{9,10},{10,1... | collective-permute-start | bytes 1966088 | tf_op jit(solution)/shard_map/ppermute | solution.py:16
  150.9 15.6 %collective-permute-done.9 = bf16[1,320,1024]{2,1,0:T(8,128)(2,1)S(1)} collective-permute-done((bf16[1,320,1024]{2,1,0:T(8,128)(2,1)S(1)}, bf16[1,320,1024]{2,1,0:T(8,128)(2,1)S(1)}, u32[]{:S(2)}, u32[]{:S(2)}) %collective-permute-start.9) | collective-permute-done | bytes 655392 | tf_op jit(solution)/shard_map/ppermute | solution.py:28
  170.3 6.6 %collective-permute-done.7 = bf16[1,320,1024]{2,1,0:T(8,128)(2,1)} collective-permute-done((bf16[1,320,1024]{2,1,0:T(8,128)(2,1)S(1)}, bf16[1,320,1024]{2,1,0:T(8,128)(2,1)}, u32[]{:S(2)}, u32[]{:S(2)}) %collective-permute-start.7) | collective-permute-done | bytes 655392 | tf_op jit(solution)/shard_map/ppermute | solution.py:16
  184.7 5.9 %collective-permute-done.10 = bf16[1,320,1024]{2,1,0:T(8,128)(2,1)S(1)} collective-permute-done((bf16[1,320,1024]{2,1,0:T(8,128)(2,1)}, bf16[1,320,1024]{2,1,0:T(8,128)(2,1)S(1)}, u32[]{:S(2)}, u32[]{:S(2)}) %collective-permute-start.10) | collective-permute-done | bytes 655392 | tf_op jit(solution)/shard_map/ppermute | solution.py:28
  193.4 6.4 %collective-permute-start.11 = (bf16[1,320,1024]{2,1,0:T(8,128)(2,1)S(1)}, bf16[1,320,1024]{2,1,0:T(8,128)(2,1)}, u32[]{:S(2)}, u32[]{:S(2)}) collective-permute-start(bf16[1,320,1024]{2,1,0:T(8,128)(2,1)S(1)} %fusion.60), channel_id=1, source_target_pairs={{0,1},{1,2},{2,3},{3,4},{4,5},{5,6},{6,7},{7,8},{8,9},{9,10},{10,1... | collective-permute-start | bytes 1966088 | tf_op jit(solution)/shard_map/ppermute | solution.py:16
  199.8 15.5 %collective-permute-done.13 = bf16[1,320,1024]{2,1,0:T(8,128)(2,1)S(1)} collective-permute-done((bf16[1,320,1024]{2,1,0:T(8,128)(2,1)S(1)}, bf16[1,320,1024]{2,1,0:T(8,128)(2,1)S(1)}, u32[]{:S(2)}, u32[]{:S(2)}) %collective-permute-start.13) | collective-permute-done | bytes 655392 | tf_op jit(solution)/shard_map/ppermute | solution.py:28
  232.9 5.6 %collective-permute-done.14 = bf16[1,320,1024]{2,1,0:T(8,128)(2,1)S(1)} collective-permute-done((bf16[1,320,1024]{2,1,0:T(8,128)(2,1)S(1)}, bf16[1,320,1024]{2,1,0:T(8,128)(2,1)S(1)}, u32[]{:S(2)}, u32[]{:S(2)}) %collective-permute-start.14) | collective-permute-done | bytes 655392 | tf_op jit(solution)/shard_map/ppermute | solution.py:28
  240.2 7.3 %collective-permute-start.15 = (bf16[1,320,1024]{2,1,0:T(8,128)(2,1)S(1)}, bf16[1,320,1024]{2,1,0:T(8,128)(2,1)}, u32[]{:S(2)}, u32[]{:S(2)}) collective-permute-start(bf16[1,320,1024]{2,1,0:T(8,128)(2,1)S(1)} %fusion.63), channel_id=1, source_target_pairs={{0,1},{1,2},{2,3},{3,4},{4,5},{5,6},{6,7},{7,8},{8,9},{9,10},{10,1... | collective-permute-start | bytes 1966088 | tf_op jit(solution)/shard_map/ppermute | solution.py:16
  247.5 9.7 %collective-permute-done.17 = bf16[1,320,1024]{2,1,0:T(8,128)(2,1)S(1)} collective-permute-done((bf16[1,320,1024]{2,1,0:T(8,128)(2,1)S(1)}, bf16[1,320,1024]{2,1,0:T(8,128)(2,1)S(1)}, u32[]{:S(2)}, u32[]{:S(2)}) %collective-permute-start.17) | collective-permute-done | bytes 655392 | tf_op jit(solution)/shard_map/ppermute | solution.py:28
  263.6 10.0 %collective-permute-done.15 = bf16[1,320,1024]{2,1,0:T(8,128)(2,1)} collective-permute-done((bf16[1,320,1024]{2,1,0:T(8,128)(2,1)S(1)}, bf16[1,320,1024]{2,1,0:T(8,128)(2,1)}, u32[]{:S(2)}, u32[]{:S(2)}) %collective-permute-start.15) | collective-permute-done | bytes 655392 | tf_op jit(solution)/shard_map/ppermute | solution.py:16
  281.3 5.9 %collective-permute-done.18 = bf16[1,320,1024]{2,1,0:T(8,128)(2,1)S(1)} collective-permute-done((bf16[1,320,1024]{2,1,0:T(8,128)(2,1)}, bf16[1,320,1024]{2,1,0:T(8,128)(2,1)S(1)}, u32[]{:S(2)}, u32[]{:S(2)}) %collective-permute-start.18) | collective-permute-done | bytes 655392 | tf_op jit(solution)/shard_map/ppermute | solution.py:28
  289.0 11.8 %collective-permute-start.19 = (bf16[1,320,1024]{2,1,0:T(8,128)(2,1)S(1)}, bf16[1,320,1024]{2,1,0:T(8,128)(2,1)}, u32[]{:S(2)}, u32[]{:S(2)}) collective-permute-start(bf16[1,320,1024]{2,1,0:T(8,128)(2,1)S(1)} %fusion.66), channel_id=1, source_target_pairs={{0,1},{1,2},{2,3},{3,4},{4,5},{5,6},{6,7},{7,8},{8,9},{9,10},{10,1... | collective-permute-start | bytes 1966088 | tf_op jit(solution)/shard_map/ppermute | solution.py:16
  305.1 9.7 %collective-permute-done.20 = bf16[1,320,1024]{2,1,0:T(8,128)(2,1)S(1)} collective-permute-done((bf16[1,320,1024]{2,1,0:T(8,128)(2,1)S(1)}, bf16[1,320,1024]{2,1,0:T(8,128)(2,1)S(1)}, u32[]{:S(2)}, u32[]{:S(2)}) %collective-permute-start.20) | collective-permute-done | bytes 655392 | tf_op jit(solution)/shard_map/ppermute | solution.py:18
  323.8 10.7 %collective-permute-done.22 = bf16[1,320,1024]{2,1,0:T(8,128)(2,1)S(1)} collective-permute-done((bf16[1,320,1024]{2,1,0:T(8,128)(2,1)S(1)}, bf16[1,320,1024]{2,1,0:T(8,128)(2,1)S(1)}, u32[]{:S(2)}, u32[]{:S(2)}) %collective-permute-start.22) | collective-permute-done | bytes 655392 | tf_op jit(solution)/shard_map/ppermute | solution.py:28
  336.2 18.9 %collective-permute-start.23 = (bf16[1,320,1024]{2,1,0:T(8,128)(2,1)S(1)}, bf16[1,320,1024]{2,1,0:T(8,128)(2,1)}, u32[]{:S(2)}, u32[]{:S(2)}) collective-permute-start(bf16[1,320,1024]{2,1,0:T(8,128)(2,1)S(1)} %fusion.69), channel_id=1, source_target_pairs={{0,1},{1,2},{2,3},{3,4},{4,5},{5,6},{6,7},{7,8},{8,9},{9,10},{10,1... | collective-permute-start | bytes 1966088 | tf_op jit(solution)/shard_map/ppermute | solution.py:16
  358.4 11.1 %collective-permute-done.24 = bf16[1,320,1024]{2,1,0:T(8,128)(2,1)S(1)} collective-permute-done((bf16[1,320,1024]{2,1,0:T(8,128)(2,1)S(1)}, bf16[1,320,1024]{2,1,0:T(8,128)(2,1)S(1)}, u32[]{:S(2)}, u32[]{:S(2)}) %collective-permute-start.24) | collective-permute-done | bytes 655392 | tf_op jit(solution)/shard_map/ppermute | solution.py:18
  383.3 63.1 %reduce-scatter.2.cloned.1.call-done = bf16[1,1,320,1024]{3,2,1,0:T(8,128)(2,1)} async-done(((bf16[4,1,320,1024]{3,2,1,0:T(8,128)(2,1)}), bf16[1,1,320,1024]{3,2,1,0:T(8,128)(2,1)}) %reduce-scatter.2.cloned.1.call-update) | async-done | bytes 655376 | tf_op jit(solution)/shard_map/reduce_scatter | solution.py:98
  (111 shorter events, 128.9 us)
Async XLA Ops:
  6.5 39.0 %all-gather.2.cloned.1.call-start = ((), (), s32[]{:S(2)}) async-start(), calls=%async_computation.1 | async-start | bytes 3276800 | tf_op jit(solution)/shard_map/all_gather | solution.py:64
  7.3 439.2 %reduce-scatter.2.cloned.1.call-start = ((), (), s32[]{:S(2)}) async-start(), calls=%async_computation.2 | async-start | bytes 3276800 | tf_op jit(solution)/shard_map/reduce_scatter | solution.py:98
  47.1 18.0 %collective-permute-start.1 = (bf16[1,320,1024]{2,1,0:T(8,128)(2,1)S(1)}, bf16[1,320,1024]{2,1,0:T(8,128)(2,1)S(1)}, u32[]{:S(2)}, u32[]{:S(2)}) collective-permute-start(bf16[1,320,1024]{2,1,0:T(8,128)(2,1)S(1)} %fusion.51), channel_id=1, source_target_pairs={{1,0},{2,1},{3,2},{4,3},{5,4},{6,5},{7,6},{8,7},{9,8},{10,9},{11,1... | collective-permute-start | bytes 1966088 | tf_op jit(solution)/shard_map/ppermute | solution.py:18
  48.7 30.0 %collective-permute-start = (bf16[1,320,1024]{2,1,0:T(8,128)(2,1)S(1)}, bf16[1,320,1024]{2,1,0:T(8,128)(2,1)}, u32[]{:S(2)}, u32[]{:S(2)}) collective-permute-start(bf16[1,320,1024]{2,1,0:T(8,128)(2,1)S(1)} %fusion.51), channel_id=1, source_target_pairs={{0,1},{1,2},{2,3},{3,4},{4,5},{5,6},{6,7},{7,8},{8,9},{9,10},{10,1... | collective-permute-start | bytes 1966088 | tf_op jit(solution)/shard_map/ppermute | solution.py:16
  82.2 11.5 %collective-permute-start.2 = (bf16[1,320,1024]{2,1,0:T(8,128)(2,1)S(1)}, bf16[1,320,1024]{2,1,0:T(8,128)(2,1)S(1)}, u32[]{:S(2)}, u32[]{:S(2)}) collective-permute-start(bf16[1,320,1024]{2,1,0:T(8,128)(2,1)S(1)} %fusion.48), channel_id=1, source_target_pairs={{0,64},{64,128},{128,192},{1,65},{65,129},{129,193},{2,66},{66,130... | collective-permute-start | bytes 1966088 | tf_op jit(solution)/shard_map/ppermute | solution.py:28
  86.3 33.4 %collective-permute-start.5 = (bf16[1,320,1024]{2,1,0:T(8,128)(2,1)S(1)}, bf16[1,320,1024]{2,1,0:T(8,128)(2,1)S(1)}, u32[]{:S(2)}, u32[]{:S(2)}) collective-permute-start(bf16[1,320,1024]{2,1,0:T(8,128)(2,1)S(1)} %get-tuple-element.23), channel_id=1, source_target_pairs={{0,64},{64,128},{128,192},{1,65},{65,129},{129,193},{2,66},{66,130... | collective-permute-start | bytes 1966088 | tf_op jit(solution)/shard_map/ppermute | solution.py:28
  95.4 27.7 %collective-permute-start.4 = (bf16[1,320,1024]{2,1,0:T(8,128)(2,1)S(1)}, bf16[1,320,1024]{2,1,0:T(8,128)(2,1)S(1)}, u32[]{:S(2)}, u32[]{:S(2)}) collective-permute-start(bf16[1,320,1024]{2,1,0:T(8,128)(2,1)S(1)} %fusion.54), channel_id=1, source_target_pairs={{1,0},{2,1},{3,2},{4,3},{5,4},{6,5},{7,6},{8,7},{9,8},{10,9},{11,1... | collective-permute-start | bytes 1966088 | tf_op jit(solution)/shard_map/ppermute | solution.py:18
  96.7 32.2 %collective-permute-start.3 = (bf16[1,320,1024]{2,1,0:T(8,128)(2,1)S(1)}, bf16[1,320,1024]{2,1,0:T(8,128)(2,1)}, u32[]{:S(2)}, u32[]{:S(2)}) collective-permute-start(bf16[1,320,1024]{2,1,0:T(8,128)(2,1)S(1)} %fusion.54), channel_id=1, source_target_pairs={{0,1},{1,2},{2,3},{3,4},{4,5},{5,6},{6,7},{7,8},{8,9},{9,10},{10,1... | collective-permute-start | bytes 1966088 | tf_op jit(solution)/shard_map/ppermute | solution.py:16
  134.3 32.2 %collective-permute-start.9 = (bf16[1,320,1024]{2,1,0:T(8,128)(2,1)S(1)}, bf16[1,320,1024]{2,1,0:T(8,128)(2,1)S(1)}, u32[]{:S(2)}, u32[]{:S(2)}) collective-permute-start(bf16[1,320,1024]{2,1,0:T(8,128)(2,1)S(1)} %get-tuple-element.21), channel_id=1, source_target_pairs={{0,64},{64,128},{128,192},{1,65},{65,129},{129,193},{2,66},{66,130... | collective-permute-start | bytes 1966088 | tf_op jit(solution)/shard_map/ppermute | solution.py:28
  143.4 25.3 %collective-permute-start.8 = (bf16[1,320,1024]{2,1,0:T(8,128)(2,1)S(1)}, bf16[1,320,1024]{2,1,0:T(8,128)(2,1)S(1)}, u32[]{:S(2)}, u32[]{:S(2)}) collective-permute-start(bf16[1,320,1024]{2,1,0:T(8,128)(2,1)S(1)} %fusion.57), channel_id=1, source_target_pairs={{1,0},{2,1},{3,2},{4,3},{5,4},{6,5},{7,6},{8,7},{9,8},{10,9},{11,1... | collective-permute-start | bytes 1966088 | tf_op jit(solution)/shard_map/ppermute | solution.py:18
  144.7 32.2 %collective-permute-start.7 = (bf16[1,320,1024]{2,1,0:T(8,128)(2,1)S(1)}, bf16[1,320,1024]{2,1,0:T(8,128)(2,1)}, u32[]{:S(2)}, u32[]{:S(2)}) collective-permute-start(bf16[1,320,1024]{2,1,0:T(8,128)(2,1)S(1)} %fusion.57), channel_id=1, source_target_pairs={{0,1},{1,2},{2,3},{3,4},{4,5},{5,6},{6,7},{7,8},{8,9},{9,10},{10,1... | collective-permute-start | bytes 1966088 | tf_op jit(solution)/shard_map/ppermute | solution.py:16
  182.7 32.6 %collective-permute-start.13 = (bf16[1,320,1024]{2,1,0:T(8,128)(2,1)S(1)}, bf16[1,320,1024]{2,1,0:T(8,128)(2,1)S(1)}, u32[]{:S(2)}, u32[]{:S(2)}) collective-permute-start(bf16[1,320,1024]{2,1,0:T(8,128)(2,1)S(1)} %get-tuple-element.19), channel_id=1, source_target_pairs={{0,64},{64,128},{128,192},{1,65},{65,129},{129,193},{2,66},{66,130... | collective-permute-start | bytes 1966088 | tf_op jit(solution)/shard_map/ppermute | solution.py:28
  192.1 27.6 %collective-permute-start.12 = (bf16[1,320,1024]{2,1,0:T(8,128)(2,1)S(1)}, bf16[1,320,1024]{2,1,0:T(8,128)(2,1)S(1)}, u32[]{:S(2)}, u32[]{:S(2)}) collective-permute-start(bf16[1,320,1024]{2,1,0:T(8,128)(2,1)S(1)} %fusion.60), channel_id=1, source_target_pairs={{1,0},{2,1},{3,2},{4,3},{5,4},{6,5},{7,6},{8,7},{9,8},{10,9},{11,1... | collective-permute-start | bytes 1966088 | tf_op jit(solution)/shard_map/ppermute | solution.py:18
  193.4 32.1 %collective-permute-start.11 = (bf16[1,320,1024]{2,1,0:T(8,128)(2,1)S(1)}, bf16[1,320,1024]{2,1,0:T(8,128)(2,1)}, u32[]{:S(2)}, u32[]{:S(2)}) collective-permute-start(bf16[1,320,1024]{2,1,0:T(8,128)(2,1)S(1)} %fusion.60), channel_id=1, source_target_pairs={{0,1},{1,2},{2,3},{3,4},{4,5},{5,6},{6,7},{7,8},{8,9},{9,10},{10,1... | collective-permute-start | bytes 1966088 | tf_op jit(solution)/shard_map/ppermute | solution.py:16
  231.0 26.3 %collective-permute-start.17 = (bf16[1,320,1024]{2,1,0:T(8,128)(2,1)S(1)}, bf16[1,320,1024]{2,1,0:T(8,128)(2,1)S(1)}, u32[]{:S(2)}, u32[]{:S(2)}) collective-permute-start(bf16[1,320,1024]{2,1,0:T(8,128)(2,1)S(1)} %get-tuple-element.17), channel_id=1, source_target_pairs={{0,64},{64,128},{128,192},{1,65},{65,129},{129,193},{2,66},{66,130... | collective-permute-start | bytes 1966088 | tf_op jit(solution)/shard_map/ppermute | solution.py:28
  238.9 23.1 %collective-permute-start.16 = (bf16[1,320,1024]{2,1,0:T(8,128)(2,1)S(1)}, bf16[1,320,1024]{2,1,0:T(8,128)(2,1)S(1)}, u32[]{:S(2)}, u32[]{:S(2)}) collective-permute-start(bf16[1,320,1024]{2,1,0:T(8,128)(2,1)S(1)} %fusion.63), channel_id=1, source_target_pairs={{1,0},{2,1},{3,2},{4,3},{5,4},{6,5},{7,6},{8,7},{9,8},{10,9},{11,1... | collective-permute-start | bytes 1966088 | tf_op jit(solution)/shard_map/ppermute | solution.py:18
  240.2 33.4 %collective-permute-start.15 = (bf16[1,320,1024]{2,1,0:T(8,128)(2,1)S(1)}, bf16[1,320,1024]{2,1,0:T(8,128)(2,1)}, u32[]{:S(2)}, u32[]{:S(2)}) collective-permute-start(bf16[1,320,1024]{2,1,0:T(8,128)(2,1)S(1)} %fusion.63), channel_id=1, source_target_pairs={{0,1},{1,2},{2,3},{3,4},{4,5},{5,6},{6,7},{7,8},{8,9},{9,10},{10,1... | collective-permute-start | bytes 1966088 | tf_op jit(solution)/shard_map/ppermute | solution.py:16
  279.4 21.3 %collective-permute-start.21 = (bf16[1,320,1024]{2,1,0:T(8,128)(2,1)S(1)}, bf16[1,320,1024]{2,1,0:T(8,128)(2,1)S(1)}, u32[]{:S(2)}, u32[]{:S(2)}) collective-permute-start(bf16[1,320,1024]{2,1,0:T(8,128)(2,1)S(1)} %get-tuple-element.15), channel_id=1, source_target_pairs={{0,64},{64,128},{128,192},{1,65},{65,129},{129,193},{2,66},{66,130... | collective-permute-start | bytes 1966088 | tf_op jit(solution)/shard_map/ppermute | solution.py:28
  287.6 27.2 %collective-permute-start.20 = (bf16[1,320,1024]{2,1,0:T(8,128)(2,1)S(1)}, bf16[1,320,1024]{2,1,0:T(8,128)(2,1)S(1)}, u32[]{:S(2)}, u32[]{:S(2)}) collective-permute-start(bf16[1,320,1024]{2,1,0:T(8,128)(2,1)S(1)} %fusion.66), channel_id=1, source_target_pairs={{1,0},{2,1},{3,2},{4,3},{5,4},{6,5},{7,6},{8,7},{9,8},{10,9},{11,1... | collective-permute-start | bytes 1966088 | tf_op jit(solution)/shard_map/ppermute | solution.py:18
  289.0 27.5 %collective-permute-start.19 = (bf16[1,320,1024]{2,1,0:T(8,128)(2,1)S(1)}, bf16[1,320,1024]{2,1,0:T(8,128)(2,1)}, u32[]{:S(2)}, u32[]{:S(2)}) collective-permute-start(bf16[1,320,1024]{2,1,0:T(8,128)(2,1)S(1)} %fusion.66), channel_id=1, source_target_pairs={{0,1},{1,2},{2,3},{3,4},{4,5},{5,6},{6,7},{7,8},{8,9},{9,10},{10,1... | collective-permute-start | bytes 1966088 | tf_op jit(solution)/shard_map/ppermute | solution.py:16
  320.0 14.5 %collective-permute-start.22 = (bf16[1,320,1024]{2,1,0:T(8,128)(2,1)S(1)}, bf16[1,320,1024]{2,1,0:T(8,128)(2,1)S(1)}, u32[]{:S(2)}, u32[]{:S(2)}) collective-permute-start(bf16[1,320,1024]{2,1,0:T(8,128)(2,1)S(1)} %fusion.43), channel_id=1, source_target_pairs={{0,64},{64,128},{128,192},{1,65},{65,129},{129,193},{2,66},{66,130... | collective-permute-start | bytes 1966088 | tf_op jit(solution)/shard_map/ppermute | solution.py:28
  321.9 33.2 %collective-permute-start.25 = (bf16[1,320,1024]{2,1,0:T(8,128)(2,1)S(1)}, bf16[1,320,1024]{2,1,0:T(8,128)(2,1)S(1)}, u32[]{:S(2)}, u32[]{:S(2)}) collective-permute-start(bf16[1,320,1024]{2,1,0:T(8,128)(2,1)S(1)} %get-tuple-element.13), channel_id=1, source_target_pairs={{0,64},{64,128},{128,192},{1,65},{65,129},{129,193},{2,66},{66,130... | collective-permute-start | bytes 1966088 | tf_op jit(solution)/shard_map/ppermute | solution.py:28
  334.9 34.6 %collective-permute-start.24 = (bf16[1,320,1024]{2,1,0:T(8,128)(2,1)S(1)}, bf16[1,320,1024]{2,1,0:T(8,128)(2,1)S(1)}, u32[]{:S(2)}, u32[]{:S(2)}) collective-permute-start(bf16[1,320,1024]{2,1,0:T(8,128)(2,1)S(1)} %fusion.69), channel_id=1, source_target_pairs={{1,0},{2,1},{3,2},{4,3},{5,4},{6,5},{7,6},{8,7},{9,8},{10,9},{11,1... | collective-permute-start | bytes 1966088 | tf_op jit(solution)/shard_map/ppermute | solution.py:18
  336.2 40.1 %collective-permute-start.23 = (bf16[1,320,1024]{2,1,0:T(8,128)(2,1)S(1)}, bf16[1,320,1024]{2,1,0:T(8,128)(2,1)}, u32[]{:S(2)}, u32[]{:S(2)}) collective-permute-start(bf16[1,320,1024]{2,1,0:T(8,128)(2,1)S(1)} %fusion.69), channel_id=1, source_target_pairs={{0,1},{1,2},{2,3},{3,4},{4,5},{5,6},{6,7},{7,8},{8,9},{9,10},{10,1... | collective-permute-start | bytes 1966088 | tf_op jit(solution)/shard_map/ppermute | solution.py:16
  (9 other events, 231.6 us)
Sparse Core Ops, SparseCore 0:
  9.2 36.3 all-gather.1
  383.5 62.9 reduce-scatter.1
where the time goes:
time: 455 us; the launch traced here: 453 us
  waiting for transfers between devices  270 us (59%)
  starting transfers between devices  95.6 us (21%)
  matrix products  60.9 us (13%)
  between operations  13.9 us (3%)
  other arithmetic  12.4 us (3%)
    ppermute x12, waiting for transfers between devices, shifted(): return lax.ppermute(array, axis, pairs)  97.1 us
    reduce_scatter x1, waiting for transfers between devices, shards(): lax.psum_scatter(stacked.astype(jnp.bfloat16), 'segment', scatter_dimensi...  63.1 us
    ppermute x7, starting transfers between devices, extended(): lax.ppermute(tail, axis, [(i, (i + 1) % count) for i in range(ends)])  61.4 us
    dot_general x28, matrix products, channel_mix(): jnp.einsum('io,fip->fop', weight, field, preferred_element_type=jnp.float32)  60.7 us
    ppermute x7, waiting for transfers between devices, extended(): lax.ppermute(tail, axis, [(i, (i + 1) % count) for i in range(ends)])  42.2 us
    all_gather x1, waiting for transfers between devices, shards(): all_clips = lax.all_gather(clips, 'segment', axis=0, tiled=True)  35.6 us
    ppermute x7, waiting for transfers between devices, extended(): lax.ppermute(head, axis, [((i + 1) % count, i) for i in range(ends)])  31.1 us
    ppermute x12, starting transfers between devices, shifted(): return lax.ppermute(array, axis, pairs)  25.2 us
  transfers between devices with their start and end apart: 28, of which 22 were waited for; matrix products, arithmetic and copies ran while one was open for 10% of the time, Pallas kernels for 0%

commit v1 on v0

--- a/solution.py
+++ b/solution.py
@@ -61,7 +61,9 @@
     sections = lax.axis_size("segment")
     section = lax.axis_index("segment")
     emb = embed(timesteps, clips.shape[2])
-    all_clips = lax.all_gather(clips, "segment", axis=0, tiled=True)
+    all_clips = jnp.concatenate(
+        lax.all_to_all(jnp.stack([clips] * lax.axis_size("segment")), "segment", 0, 0), axis=0
+    )
     batches = all_clips.shape[0]
     film_all = jnp.dot(emb, film_weight[0], preferred_element_type=jnp.float32)
     own_gain = lax.dynamic_index_in_dim(gain, section, 0, keepdims=False)

time: 455 us -> 459 us (level)
  starting transfers between devices: 95.6 us -> 103 us
    all_gather x1 -> x0, waiting for transfers between devices: 35.6 us -> none  [shards(): all_clips = lax.all_gather(clips, 'segment', axis=0, tiled=True)]
    all_to_all x0 -> x1, waiting for transfers between devices: none -> 31.1 us  [shards(): lax.all_to_all(jnp.stack([clips] * lax.axis_size('segment')), 'segment',...]
    all_to_all x0 -> x1, starting transfers between devices: none -> 7.88 us  [shards(): lax.all_to_all(jnp.stack([clips] * lax.axis_size('segment')), 'segment',...]
    reduce_scatter x1, waiting for transfers between devices: 63.1 us -> 70.3 us  [shards(): lax.psum_scatter(stacked.astype(jnp.bfloat16), 'segment', scatter_dimensi...]
    ppermute x7, waiting for transfers between devices: 42.2 us -> 37 us  [extended(): lax.ppermute(tail, axis, [(i, (i + 1) % count) for i in range(ends)])]
  transfers between devices with their start and end apart: 28 -> 28, of which waited for: 22 -> 21; matrix products, arithmetic and copies ran while one was open for 10% -> 9% of each run, Pallas kernels for 0% -> 0%
where the time goes in v1:
time: 459 us; the launch traced here: 458 us
  waiting for transfers between devices  266 us (58%)
  starting transfers between devices  103 us (22%)
  matrix products  60.8 us (13%)
  between operations  13.9 us (3%)
  other arithmetic  10.7 us (2%)
    ppermute x12, waiting for transfers between devices, shifted(): return lax.ppermute(array, axis, pairs)  97.2 us
    reduce_scatter x1, waiting for transfers between devices, shards(): lax.psum_scatter(stacked.astype(jnp.bfloat16), 'segment', scatter_dimensi...  70.3 us
    ppermute x7, starting transfers between devices, extended(): lax.ppermute(tail, axis, [(i, (i + 1) % count) for i in range(ends)])  61.5 us
    dot_general x28, matrix products, channel_mix(): jnp.einsum('io,fip->fop', weight, field, preferred_element_type=jnp.float32)  60.6 us
    ppermute x7, waiting for transfers between devices, extended(): lax.ppermute(tail, axis, [(i, (i + 1) % count) for i in range(ends)])  37 us
    all_to_all x1, waiting for transfers between devices, shards(): lax.all_to_all(jnp.stack([clips] * lax.axis_size('segment')), 'segment',...  31.1 us
    ppermute x7, waiting for transfers between devices, extended(): lax.ppermute(head, axis, [((i + 1) % count, i) for i in range(ends)])  30.4 us
    ppermute x12, starting transfers between devices, shifted(): return lax.ppermute(array, axis, pairs)  24.3 us
  transfers between devices with their start and end apart: 28, of which 21 were waited for; matrix products, arithmetic and copies ran while one was open for 9% of the time, Pallas kernels for 0%

profile of v1, /device:TPU:1, one launch (start us, length us, event | category | flops | bytes accessed | tf_op | source)
XLA Modules:
  0.0 457.8 jit_solution(9121674600165378628)
XLA Ops:
  9.5 7.9 %all-to-all-start = ((bf16[4,1,1,320,1024]{4,3,2,1,0:T(8,128)(2,1)}), bf16[4,1,1,320,1024]{4,3,2,1,0:T(8,128)(2,1)}, u32[]{:S(2)}, u32[]{:S(2)}) async-start(bf16[4,1,1,320,1024]{4,3,2,1,0:T(8,128)(2,1)} %stack.22), calls=%async_computation | async-start | bytes 5242880 | tf_op jit(solution)/shard_map/all_to_all | solution.py:65
  18.4 31.1 %all-to-all-done = bf16[4,1,1,320,1024]{4,3,2,1,0:T(8,128)(2,1)} async-done(((bf16[4,1,1,320,1024]{4,3,2,1,0:T(8,128)(2,1)}), bf16[4,1,1,320,1024]{4,3,2,1,0:T(8,128)(2,1)}, u32[]{:S(2)}, u32[]{:S(2)}) %all-to-all-start) | async-done | bytes 2621472 | tf_op jit(solution)/shard_map/all_to_all | solution.py:65
  60.2 8.1 %collective-permute-done.1 = bf16[1,320,1024]{2,1,0:T(8,128)(2,1)S(1)} collective-permute-done((bf16[1,320,1024]{2,1,0:T(8,128)(2,1)S(1)}, bf16[1,320,1024]{2,1,0:T(8,128)(2,1)S(1)}, u32[]{:S(2)}, u32[]{:S(2)}) %collective-permute-start.1) | collective-permute-done | bytes 655392 | tf_op jit(solution)/shard_map/ppermute | solution.py:18
  69.9 12.0 %collective-permute-done = bf16[1,320,1024]{2,1,0:T(8,128)(2,1)} collective-permute-done((bf16[1,320,1024]{2,1,0:T(8,128)(2,1)S(1)}, bf16[1,320,1024]{2,1,0:T(8,128)(2,1)}, u32[]{:S(2)}, u32[]{:S(2)}) %collective-permute-start) | collective-permute-done | bytes 655392 | tf_op jit(solution)/shard_map/ppermute | solution.py:16
  90.6 5.6 %collective-permute-done.2 = bf16[1,320,1024]{2,1,0:T(8,128)(2,1)S(1)} collective-permute-done((bf16[1,320,1024]{2,1,0:T(8,128)(2,1)S(1)}, bf16[1,320,1024]{2,1,0:T(8,128)(2,1)S(1)}, u32[]{:S(2)}, u32[]{:S(2)}) %collective-permute-start.2) | collective-permute-done | bytes 655392 | tf_op jit(solution)/shard_map/ppermute | solution.py:28
  99.0 5.9 %collective-permute-start.3 = (bf16[1,320,1024]{2,1,0:T(8,128)(2,1)S(1)}, bf16[1,320,1024]{2,1,0:T(8,128)(2,1)}, u32[]{:S(2)}, u32[]{:S(2)}) collective-permute-start(bf16[1,320,1024]{2,1,0:T(8,128)(2,1)S(1)} %fusion.54), channel_id=1, source_target_pairs={{0,1},{1,2},{2,3},{3,4},{4,5},{5,6},{6,7},{7,8},{8,9},{9,10},{10,1... | collective-permute-start | bytes 1966088 | tf_op jit(solution)/shard_map/ppermute | solution.py:16
  104.9 17.2 %collective-permute-done.5 = bf16[1,320,1024]{2,1,0:T(8,128)(2,1)S(1)} collective-permute-done((bf16[1,320,1024]{2,1,0:T(8,128)(2,1)S(1)}, bf16[1,320,1024]{2,1,0:T(8,128)(2,1)S(1)}, u32[]{:S(2)}, u32[]{:S(2)}) %collective-permute-start.5) | collective-permute-done | bytes 655392 | tf_op jit(solution)/shard_map/ppermute | solution.py:28
  138.6 5.6 %collective-permute-done.6 = bf16[1,320,1024]{2,1,0:T(8,128)(2,1)S(1)} collective-permute-done((bf16[1,320,1024]{2,1,0:T(8,128)(2,1)S(1)}, bf16[1,320,1024]{2,1,0:T(8,128)(2,1)S(1)}, u32[]{:S(2)}, u32[]{:S(2)}) %collective-permute-start.6) | collective-permute-done | bytes 655392 | tf_op jit(solution)/shard_map/ppermute | solution.py:28
  147.0 6.2 %collective-permute-start.7 = (bf16[1,320,1024]{2,1,0:T(8,128)(2,1)S(1)}, bf16[1,320,1024]{2,1,0:T(8,128)(2,1)}, u32[]{:S(2)}, u32[]{:S(2)}) collective-permute-start(bf16[1,320,1024]{2,1,0:T(8,128)(2,1)S(1)} %fusion.57), channel_id=1, source_target_pairs={{0,1},{1,2},{2,3},{3,4},{4,5},{5,6},{6,7},{7,8},{8,9},{9,10},{10,1... | collective-permute-start | bytes 1966088 | tf_op jit(solution)/shard_map/ppermute | solution.py:16
  153.2 15.6 %collective-permute-done.9 = bf16[1,320,1024]{2,1,0:T(8,128)(2,1)S(1)} collective-permute-done((bf16[1,320,1024]{2,1,0:T(8,128)(2,1)S(1)}, bf16[1,320,1024]{2,1,0:T(8,128)(2,1)S(1)}, u32[]{:S(2)}, u32[]{:S(2)}) %collective-permute-start.9) | collective-permute-done | bytes 655392 | tf_op jit(solution)/shard_map/ppermute | solution.py:28
  172.7 6.6 %collective-permute-done.7 = bf16[1,320,1024]{2,1,0:T(8,128)(2,1)} collective-permute-done((bf16[1,320,1024]{2,1,0:T(8,128)(2,1)S(1)}, bf16[1,320,1024]{2,1,0:T(8,128)(2,1)}, u32[]{:S(2)}, u32[]{:S(2)}) %collective-permute-start.7) | collective-permute-done | bytes 655392 | tf_op jit(solution)/shard_map/ppermute | solution.py:16
  187.0 5.9 %collective-permute-done.10 = bf16[1,320,1024]{2,1,0:T(8,128)(2,1)S(1)} collective-permute-done((bf16[1,320,1024]{2,1,0:T(8,128)(2,1)}, bf16[1,320,1024]{2,1,0:T(8,128)(2,1)S(1)}, u32[]{:S(2)}, u32[]{:S(2)}) %collective-permute-start.10) | collective-permute-done | bytes 655392 | tf_op jit(solution)/shard_map/ppermute | solution.py:28
  195.8 6.4 %collective-permute-start.11 = (bf16[1,320,1024]{2,1,0:T(8,128)(2,1)S(1)}, bf16[1,320,1024]{2,1,0:T(8,128)(2,1)}, u32[]{:S(2)}, u32[]{:S(2)}) collective-permute-start(bf16[1,320,1024]{2,1,0:T(8,128)(2,1)S(1)} %fusion.60), channel_id=1, source_target_pairs={{0,1},{1,2},{2,3},{3,4},{4,5},{5,6},{6,7},{7,8},{8,9},{9,10},{10,1... | collective-permute-start | bytes 1966088 | tf_op jit(solution)/shard_map/ppermute | solution.py:16
  202.2 15.5 %collective-permute-done.13 = bf16[1,320,1024]{2,1,0:T(8,128)(2,1)S(1)} collective-permute-done((bf16[1,320,1024]{2,1,0:T(8,128)(2,1)S(1)}, bf16[1,320,1024]{2,1,0:T(8,128)(2,1)S(1)}, u32[]{:S(2)}, u32[]{:S(2)}) %collective-permute-start.13) | collective-permute-done | bytes 655392 | tf_op jit(solution)/shard_map/ppermute | solution.py:28
  242.6 7.3 %collective-permute-start.15 = (bf16[1,320,1024]{2,1,0:T(8,128)(2,1)S(1)}, bf16[1,320,1024]{2,1,0:T(8,128)(2,1)}, u32[]{:S(2)}, u32[]{:S(2)}) collective-permute-start(bf16[1,320,1024]{2,1,0:T(8,128)(2,1)S(1)} %fusion.63), channel_id=1, source_target_pairs={{0,1},{1,2},{2,3},{3,4},{4,5},{5,6},{6,7},{7,8},{8,9},{9,10},{10,1... | collective-permute-start | bytes 1966088 | tf_op jit(solution)/shard_map/ppermute | solution.py:16
  249.9 9.7 %collective-permute-done.17 = bf16[1,320,1024]{2,1,0:T(8,128)(2,1)S(1)} collective-permute-done((bf16[1,320,1024]{2,1,0:T(8,128)(2,1)S(1)}, bf16[1,320,1024]{2,1,0:T(8,128)(2,1)S(1)}, u32[]{:S(2)}, u32[]{:S(2)}) %collective-permute-start.17) | collective-permute-done | bytes 655392 | tf_op jit(solution)/shard_map/ppermute | solution.py:28
  266.0 10.0 %collective-permute-done.15 = bf16[1,320,1024]{2,1,0:T(8,128)(2,1)} collective-permute-done((bf16[1,320,1024]{2,1,0:T(8,128)(2,1)S(1)}, bf16[1,320,1024]{2,1,0:T(8,128)(2,1)}, u32[]{:S(2)}, u32[]{:S(2)}) %collective-permute-start.15) | collective-permute-done | bytes 655392 | tf_op jit(solution)/shard_map/ppermute | solution.py:16
  283.7 5.9 %collective-permute-done.18 = bf16[1,320,1024]{2,1,0:T(8,128)(2,1)S(1)} collective-permute-done((bf16[1,320,1024]{2,1,0:T(8,128)(2,1)}, bf16[1,320,1024]{2,1,0:T(8,128)(2,1)S(1)}, u32[]{:S(2)}, u32[]{:S(2)}) %collective-permute-start.18) | collective-permute-done | bytes 655392 | tf_op jit(solution)/shard_map/ppermute | solution.py:28
  291.3 12.0 %collective-permute-start.19 = (bf16[1,320,1024]{2,1,0:T(8,128)(2,1)S(1)}, bf16[1,320,1024]{2,1,0:T(8,128)(2,1)}, u32[]{:S(2)}, u32[]{:S(2)}) collective-permute-start(bf16[1,320,1024]{2,1,0:T(8,128)(2,1)S(1)} %fusion.66), channel_id=1, source_target_pairs={{0,1},{1,2},{2,3},{3,4},{4,5},{5,6},{6,7},{7,8},{8,9},{9,10},{10,1... | collective-permute-start | bytes 1966088 | tf_op jit(solution)/shard_map/ppermute | solution.py:16
  307.7 9.7 %collective-permute-done.20 = bf16[1,320,1024]{2,1,0:T(8,128)(2,1)S(1)} collective-permute-done((bf16[1,320,1024]{2,1,0:T(8,128)(2,1)S(1)}, bf16[1,320,1024]{2,1,0:T(8,128)(2,1)S(1)}, u32[]{:S(2)}, u32[]{:S(2)}) %collective-permute-start.20) | collective-permute-done | bytes 655392 | tf_op jit(solution)/shard_map/ppermute | solution.py:18
  326.4 10.7 %collective-permute-done.22 = bf16[1,320,1024]{2,1,0:T(8,128)(2,1)S(1)} collective-permute-done((bf16[1,320,1024]{2,1,0:T(8,128)(2,1)S(1)}, bf16[1,320,1024]{2,1,0:T(8,128)(2,1)S(1)}, u32[]{:S(2)}, u32[]{:S(2)}) %collective-permute-start.22) | collective-permute-done | bytes 655392 | tf_op jit(solution)/shard_map/ppermute | solution.py:28
  338.8 18.9 %collective-permute-start.23 = (bf16[1,320,1024]{2,1,0:T(8,128)(2,1)S(1)}, bf16[1,320,1024]{2,1,0:T(8,128)(2,1)}, u32[]{:S(2)}, u32[]{:S(2)}) collective-permute-start(bf16[1,320,1024]{2,1,0:T(8,128)(2,1)S(1)} %fusion.69), channel_id=1, source_target_pairs={{0,1},{1,2},{2,3},{3,4},{4,5},{5,6},{6,7},{7,8},{8,9},{9,10},{10,1... | collective-permute-start | bytes 1966088 | tf_op jit(solution)/shard_map/ppermute | solution.py:16
  361.0 11.1 %collective-permute-done.24 = bf16[1,320,1024]{2,1,0:T(8,128)(2,1)S(1)} collective-permute-done((bf16[1,320,1024]{2,1,0:T(8,128)(2,1)S(1)}, bf16[1,320,1024]{2,1,0:T(8,128)(2,1)S(1)}, u32[]{:S(2)}, u32[]{:S(2)}) %collective-permute-start.24) | collective-permute-done | bytes 655392 | tf_op jit(solution)/shard_map/ppermute | solution.py:18
  380.7 70.3 %reduce-scatter.2.cloned.1.call-done = bf16[1,1,320,1024]{3,2,1,0:T(8,128)(2,1)} async-done(((bf16[4,1,320,1024]{3,2,1,0:T(8,128)(2,1)}), bf16[1,1,320,1024]{3,2,1,0:T(8,128)(2,1)}) %reduce-scatter.2.cloned.1.call-update) | async-done | bytes 655376 | tf_op jit(solution)/shard_map/reduce_scatter | solution.py:100
  (115 shorter events, 129.0 us)
Async XLA Ops:
  9.5 39.9 %all-to-all-start = ((bf16[4,1,1,320,1024]{4,3,2,1,0:T(8,128)(2,1)}), bf16[4,1,1,320,1024]{4,3,2,1,0:T(8,128)(2,1)}, u32[]{:S(2)}, u32[]{:S(2)}) async-start(bf16[4,1,1,320,1024]{4,3,2,1,0:T(8,128)(2,1)} %stack.22), calls=%async_computation | async-start | bytes 5242880 | tf_op jit(solution)/shard_map/all_to_all | solution.py:65
  17.4 433.6 %reduce-scatter.2.cloned.1.call-start = ((), (), s32[]{:S(2)}) async-start(), calls=%async_computation.2 | async-start | bytes 3276800 | tf_op jit(solution)/shard_map/reduce_scatter | solution.py:100
  51.0 17.3 %collective-permute-start.1 = (bf16[1,320,1024]{2,1,0:T(8,128)(2,1)S(1)}, bf16[1,320,1024]{2,1,0:T(8,128)(2,1)S(1)}, u32[]{:S(2)}, u32[]{:S(2)}) collective-permute-start(bf16[1,320,1024]{2,1,0:T(8,128)(2,1)S(1)} %fusion.51), channel_id=1, source_target_pairs={{1,0},{2,1},{3,2},{4,3},{5,4},{6,5},{7,6},{8,7},{9,8},{10,9},{11,1... | collective-permute-start | bytes 1966088 | tf_op jit(solution)/shard_map/ppermute | solution.py:18
  52.5 29.3 %collective-permute-start = (bf16[1,320,1024]{2,1,0:T(8,128)(2,1)S(1)}, bf16[1,320,1024]{2,1,0:T(8,128)(2,1)}, u32[]{:S(2)}, u32[]{:S(2)}) collective-permute-start(bf16[1,320,1024]{2,1,0:T(8,128)(2,1)S(1)} %fusion.51), channel_id=1, source_target_pairs={{0,1},{1,2},{2,3},{3,4},{4,5},{5,6},{6,7},{7,8},{8,9},{9,10},{10,1... | collective-permute-start | bytes 1966088 | tf_op jit(solution)/shard_map/ppermute | solution.py:16
  85.4 10.8 %collective-permute-start.2 = (bf16[1,320,1024]{2,1,0:T(8,128)(2,1)S(1)}, bf16[1,320,1024]{2,1,0:T(8,128)(2,1)S(1)}, u32[]{:S(2)}, u32[]{:S(2)}) collective-permute-start(bf16[1,320,1024]{2,1,0:T(8,128)(2,1)S(1)} %fusion.48), channel_id=1, source_target_pairs={{0,64},{64,128},{128,192},{1,65},{65,129},{129,193},{2,66},{66,130... | collective-permute-start | bytes 1966088 | tf_op jit(solution)/shard_map/ppermute | solution.py:28
  88.6 33.4 %collective-permute-start.5 = (bf16[1,320,1024]{2,1,0:T(8,128)(2,1)S(1)}, bf16[1,320,1024]{2,1,0:T(8,128)(2,1)S(1)}, u32[]{:S(2)}, u32[]{:S(2)}) collective-permute-start(bf16[1,320,1024]{2,1,0:T(8,128)(2,1)S(1)} %get-tuple-element.23), channel_id=1, source_target_pairs={{0,64},{64,128},{128,192},{1,65},{65,129},{129,193},{2,66},{66,130... | collective-permute-start | bytes 1966088 | tf_op jit(solution)/shard_map/ppermute | solution.py:28
  97.7 27.6 %collective-permute-start.4 = (bf16[1,320,1024]{2,1,0:T(8,128)(2,1)S(1)}, bf16[1,320,1024]{2,1,0:T(8,128)(2,1)S(1)}, u32[]{:S(2)}, u32[]{:S(2)}) collective-permute-start(bf16[1,320,1024]{2,1,0:T(8,128)(2,1)S(1)} %fusion.54), channel_id=1, source_target_pairs={{1,0},{2,1},{3,2},{4,3},{5,4},{6,5},{7,6},{8,7},{9,8},{10,9},{11,1... | collective-permute-start | bytes 1966088 | tf_op jit(solution)/shard_map/ppermute | solution.py:18
  99.0 32.2 %collective-permute-start.3 = (bf16[1,320,1024]{2,1,0:T(8,128)(2,1)S(1)}, bf16[1,320,1024]{2,1,0:T(8,128)(2,1)}, u32[]{:S(2)}, u32[]{:S(2)}) collective-permute-start(bf16[1,320,1024]{2,1,0:T(8,128)(2,1)S(1)} %fusion.54), channel_id=1, source_target_pairs={{0,1},{1,2},{2,3},{3,4},{4,5},{5,6},{6,7},{7,8},{8,9},{9,10},{10,1... | collective-permute-start | bytes 1966088 | tf_op jit(solution)/shard_map/ppermute | solution.py:16
  136.6 32.2 %collective-permute-start.9 = (bf16[1,320,1024]{2,1,0:T(8,128)(2,1)S(1)}, bf16[1,320,1024]{2,1,0:T(8,128)(2,1)S(1)}, u32[]{:S(2)}, u32[]{:S(2)}) collective-permute-start(bf16[1,320,1024]{2,1,0:T(8,128)(2,1)S(1)} %get-tuple-element.21), channel_id=1, source_target_pairs={{0,64},{64,128},{128,192},{1,65},{65,129},{129,193},{2,66},{66,130... | collective-permute-start | bytes 1966088 | tf_op jit(solution)/shard_map/ppermute | solution.py:28
  145.7 25.3 %collective-permute-start.8 = (bf16[1,320,1024]{2,1,0:T(8,128)(2,1)S(1)}, bf16[1,320,1024]{2,1,0:T(8,128)(2,1)S(1)}, u32[]{:S(2)}, u32[]{:S(2)}) collective-permute-start(bf16[1,320,1024]{2,1,0:T(8,128)(2,1)S(1)} %fusion.57), channel_id=1, source_target_pairs={{1,0},{2,1},{3,2},{4,3},{5,4},{6,5},{7,6},{8,7},{9,8},{10,9},{11,1... | collective-permute-start | bytes 1966088 | tf_op jit(solution)/shard_map/ppermute | solution.py:18
  147.0 32.2 %collective-permute-start.7 = (bf16[1,320,1024]{2,1,0:T(8,128)(2,1)S(1)}, bf16[1,320,1024]{2,1,0:T(8,128)(2,1)}, u32[]{:S(2)}, u32[]{:S(2)}) collective-permute-start(bf16[1,320,1024]{2,1,0:T(8,128)(2,1)S(1)} %fusion.57), channel_id=1, source_target_pairs={{0,1},{1,2},{2,3},{3,4},{4,5},{5,6},{6,7},{7,8},{8,9},{9,10},{10,1... | collective-permute-start | bytes 1966088 | tf_op jit(solution)/shard_map/ppermute | solution.py:16
  185.1 32.6 %collective-permute-start.13 = (bf16[1,320,1024]{2,1,0:T(8,128)(2,1)S(1)}, bf16[1,320,1024]{2,1,0:T(8,128)(2,1)S(1)}, u32[]{:S(2)}, u32[]{:S(2)}) collective-permute-start(bf16[1,320,1024]{2,1,0:T(8,128)(2,1)S(1)} %get-tuple-element.19), channel_id=1, source_target_pairs={{0,64},{64,128},{128,192},{1,65},{65,129},{129,193},{2,66},{66,130... | collective-permute-start | bytes 1966088 | tf_op jit(solution)/shard_map/ppermute | solution.py:28
  194.5 27.6 %collective-permute-start.12 = (bf16[1,320,1024]{2,1,0:T(8,128)(2,1)S(1)}, bf16[1,320,1024]{2,1,0:T(8,128)(2,1)S(1)}, u32[]{:S(2)}, u32[]{:S(2)}) collective-permute-start(bf16[1,320,1024]{2,1,0:T(8,128)(2,1)S(1)} %fusion.60), channel_id=1, source_target_pairs={{1,0},{2,1},{3,2},{4,3},{5,4},{6,5},{7,6},{8,7},{9,8},{10,9},{11,1... | collective-permute-start | bytes 1966088 | tf_op jit(solution)/shard_map/ppermute | solution.py:18
  195.8 32.1 %collective-permute-start.11 = (bf16[1,320,1024]{2,1,0:T(8,128)(2,1)S(1)}, bf16[1,320,1024]{2,1,0:T(8,128)(2,1)}, u32[]{:S(2)}, u32[]{:S(2)}) collective-permute-start(bf16[1,320,1024]{2,1,0:T(8,128)(2,1)S(1)} %fusion.60), channel_id=1, source_target_pairs={{0,1},{1,2},{2,3},{3,4},{4,5},{5,6},{6,7},{7,8},{8,9},{9,10},{10,1... | collective-permute-start | bytes 1966088 | tf_op jit(solution)/shard_map/ppermute | solution.py:16
  233.3 26.3 %collective-permute-start.17 = (bf16[1,320,1024]{2,1,0:T(8,128)(2,1)S(1)}, bf16[1,320,1024]{2,1,0:T(8,128)(2,1)S(1)}, u32[]{:S(2)}, u32[]{:S(2)}) collective-permute-start(bf16[1,320,1024]{2,1,0:T(8,128)(2,1)S(1)} %get-tuple-element.17), channel_id=1, source_target_pairs={{0,64},{64,128},{128,192},{1,65},{65,129},{129,193},{2,66},{66,130... | collective-permute-start | bytes 1966088 | tf_op jit(solution)/shard_map/ppermute | solution.py:28
  241.3 23.1 %collective-permute-start.16 = (bf16[1,320,1024]{2,1,0:T(8,128)(2,1)S(1)}, bf16[1,320,1024]{2,1,0:T(8,128)(2,1)S(1)}, u32[]{:S(2)}, u32[]{:S(2)}) collective-permute-start(bf16[1,320,1024]{2,1,0:T(8,128)(2,1)S(1)} %fusion.63), channel_id=1, source_target_pairs={{1,0},{2,1},{3,2},{4,3},{5,4},{6,5},{7,6},{8,7},{9,8},{10,9},{11,1... | collective-permute-start | bytes 1966088 | tf_op jit(solution)/shard_map/ppermute | solution.py:18
  242.6 33.4 %collective-permute-start.15 = (bf16[1,320,1024]{2,1,0:T(8,128)(2,1)S(1)}, bf16[1,320,1024]{2,1,0:T(8,128)(2,1)}, u32[]{:S(2)}, u32[]{:S(2)}) collective-permute-start(bf16[1,320,1024]{2,1,0:T(8,128)(2,1)S(1)} %fusion.63), channel_id=1, source_target_pairs={{0,1},{1,2},{2,3},{3,4},{4,5},{5,6},{6,7},{7,8},{8,9},{9,10},{10,1... | collective-permute-start | bytes 1966088 | tf_op jit(solution)/shard_map/ppermute | solution.py:16
  281.8 21.5 %collective-permute-start.21 = (bf16[1,320,1024]{2,1,0:T(8,128)(2,1)S(1)}, bf16[1,320,1024]{2,1,0:T(8,128)(2,1)S(1)}, u32[]{:S(2)}, u32[]{:S(2)}) collective-permute-start(bf16[1,320,1024]{2,1,0:T(8,128)(2,1)S(1)} %get-tuple-element.15), channel_id=1, source_target_pairs={{0,64},{64,128},{128,192},{1,65},{65,129},{129,193},{2,66},{66,130... | collective-permute-start | bytes 1966088 | tf_op jit(solution)/shard_map/ppermute | solution.py:28
  290.0 27.4 %collective-permute-start.20 = (bf16[1,320,1024]{2,1,0:T(8,128)(2,1)S(1)}, bf16[1,320,1024]{2,1,0:T(8,128)(2,1)S(1)}, u32[]{:S(2)}, u32[]{:S(2)}) collective-permute-start(bf16[1,320,1024]{2,1,0:T(8,128)(2,1)S(1)} %fusion.66), channel_id=1, source_target_pairs={{1,0},{2,1},{3,2},{4,3},{5,4},{6,5},{7,6},{8,7},{9,8},{10,9},{11,1... | collective-permute-start | bytes 1966088 | tf_op jit(solution)/shard_map/ppermute | solution.py:18
  291.3 27.7 %collective-permute-start.19 = (bf16[1,320,1024]{2,1,0:T(8,128)(2,1)S(1)}, bf16[1,320,1024]{2,1,0:T(8,128)(2,1)}, u32[]{:S(2)}, u32[]{:S(2)}) collective-permute-start(bf16[1,320,1024]{2,1,0:T(8,128)(2,1)S(1)} %fusion.66), channel_id=1, source_target_pairs={{0,1},{1,2},{2,3},{3,4},{4,5},{5,6},{6,7},{7,8},{8,9},{9,10},{10,1... | collective-permute-start | bytes 1966088 | tf_op jit(solution)/shard_map/ppermute | solution.py:16
  322.5 14.5 %collective-permute-start.22 = (bf16[1,320,1024]{2,1,0:T(8,128)(2,1)S(1)}, bf16[1,320,1024]{2,1,0:T(8,128)(2,1)S(1)}, u32[]{:S(2)}, u32[]{:S(2)}) collective-permute-start(bf16[1,320,1024]{2,1,0:T(8,128)(2,1)S(1)} %fusion.43), channel_id=1, source_target_pairs={{0,64},{64,128},{128,192},{1,65},{65,129},{129,193},{2,66},{66,130... | collective-permute-start | bytes 1966088 | tf_op jit(solution)/shard_map/ppermute | solution.py:28
  324.4 33.3 %collective-permute-start.25 = (bf16[1,320,1024]{2,1,0:T(8,128)(2,1)S(1)}, bf16[1,320,1024]{2,1,0:T(8,128)(2,1)S(1)}, u32[]{:S(2)}, u32[]{:S(2)}) collective-permute-start(bf16[1,320,1024]{2,1,0:T(8,128)(2,1)S(1)} %get-tuple-element.13), channel_id=1, source_target_pairs={{0,64},{64,128},{128,192},{1,65},{65,129},{129,193},{2,66},{66,130... | collective-permute-start | bytes 1966088 | tf_op jit(solution)/shard_map/ppermute | solution.py:28
  337.5 34.6 %collective-permute-start.24 = (bf16[1,320,1024]{2,1,0:T(8,128)(2,1)S(1)}, bf16[1,320,1024]{2,1,0:T(8,128)(2,1)S(1)}, u32[]{:S(2)}, u32[]{:S(2)}) collective-permute-start(bf16[1,320,1024]{2,1,0:T(8,128)(2,1)S(1)} %fusion.69), channel_id=1, source_target_pairs={{1,0},{2,1},{3,2},{4,3},{5,4},{6,5},{7,6},{8,7},{9,8},{10,9},{11,1... | collective-permute-start | bytes 1966088 | tf_op jit(solution)/shard_map/ppermute | solution.py:18
  338.8 34.9 %collective-permute-start.23 = (bf16[1,320,1024]{2,1,0:T(8,128)(2,1)S(1)}, bf16[1,320,1024]{2,1,0:T(8,128)(2,1)}, u32[]{:S(2)}, u32[]{:S(2)}) collective-permute-start(bf16[1,320,1024]{2,1,0:T(8,128)(2,1)S(1)} %fusion.69), channel_id=1, source_target_pairs={{0,1},{1,2},{2,3},{3,4},{4,5},{5,6},{6,7},{7,8},{8,9},{9,10},{10,1... | collective-permute-start | bytes 1966088 | tf_op jit(solution)/shard_map/ppermute | solution.py:16
  (11 other events, 242.3 us)
Sparse Core Ops, SparseCore 0:
  380.9 70.0 reduce-scatter.1
